TPU v7x, 32 devices: a whole 2x2x4 slice. The times are simulated.
32 devices in a mesh: dp: 8 (over z, x), fsdp: 4 (over y, core).
Axes of the slice: x: 2, y: 2, z: 4, core: 2. Of those that a mesh axis runs over, the one named last changes fastest.
Arguments:
- hidden: bfloat16 [512, 64, 768], P(('dp', 'fsdp')), may hold values from -6 to 6
- lengths: int32 [512], P(('dp', 'fsdp')), may hold values from 3 to 64, as said below
- cotangent: bfloat16 [512, 64, 768], P(('dp', 'fsdp')), may hold values from -6 to 6
- attgain: bfloat16 [768], P(('dp', 'fsdp')), may hold values from 0.25 to 1.75
- attshift: bfloat16 [768], P(('dp', 'fsdp')), may hold values from -2 to 2
- querymat: bfloat16 [768, 768], P(None, ('dp', 'fsdp')), may hold values from -0.21875 to 0.21875
- querybias: bfloat16 [768], P(('dp', 'fsdp')), may hold values from -2 to 2
- keymat: bfloat16 [768, 768], P(None, ('dp', 'fsdp')), may hold values from -0.21875 to 0.21875
- valuemat: bfloat16 [768, 768], P(None, ('dp', 'fsdp')), may hold values from -0.21875 to 0.21875
- valuebias: bfloat16 [768], P(('dp', 'fsdp')), may hold values from -2 to 2
- mixmat: bfloat16 [768, 768], P(None, ('dp', 'fsdp')), may hold values from -0.625 to 0.625
- mixbias: bfloat16 [768], P(('dp', 'fsdp')), may hold values from -2 to 2
- mlpgain: bfloat16 [768], P(('dp', 'fsdp')), may hold values from 0.25 to 1.75
- mlpshift: bfloat16 [768], P(('dp', 'fsdp')), may hold values from -2 to 2
- upmat_w: bfloat16 [768, 3072], P(None, ('dp', 'fsdp')), may hold values from -0.21875 to 0.21875
- upbias: bfloat16 [3072], P(('dp', 'fsdp')), may hold values from -2 to 2
- downmat: bfloat16 [3072, 768], P(None, ('dp', 'fsdp')), may hold values from -0.109375 to 0.109375
- downbias: bfloat16 [768], P(('dp', 'fsdp')), may hold values from -2 to 2
Outputs:
- block_out: bfloat16 [512, 64, 768], P(('dp', 'fsdp'))
- input_grad: float32 [512, 64, 768], P(('dp', 'fsdp'))
- attgain_grad: float32 [768], P(('dp', 'fsdp'))
- attshift_grad: float32 [768], P(('dp', 'fsdp'))
- querymat_grad: float32 [768, 768], P(None, ('dp', 'fsdp'))
- querybias_grad: float32 [768], P(('dp', 'fsdp'))
- keymat_grad: float32 [768, 768], P(None, ('dp', 'fsdp'))
- valuemat_grad: float32 [768, 768], P(None, ('dp', 'fsdp'))
- valuebias_grad: float32 [768], P(('dp', 'fsdp'))
- mixmat_grad: float32 [768, 768], P(None, ('dp', 'fsdp'))
- mixbias_grad: float32 [768], P(('dp', 'fsdp'))
- mlpgain_grad: float32 [768], P(('dp', 'fsdp'))
- mlpshift_grad: float32 [768], P(('dp', 'fsdp'))
- upmat_grad: float32 [768, 3072], P(None, ('dp', 'fsdp'))
- upbias_grad: float32 [3072], P(('dp', 'fsdp'))
- downmat_grad: float32 [3072, 768], P(None, ('dp', 'fsdp'))
- downbias_grad: float32 [768], P(('dp', 'fsdp'))
Inputs may be any that keep to these rules, and one draw needn't show every extreme that they name: The first lengths[c] token slots of caption c are real, the rest padding; some caption has 64 real tokens and some has 3.
All inputs are finite; a program needn't handle non-finite values.
Results may differ from a plain program's by a relative error of at most 0.013.
Values may be sent and summed in bfloat16 or wider, within the bound.
No kernel may reach another device: no remote copies, remote signals or barrier semaphores. Data moves between devices by JAX's collectives and lax.ppermute only.
A program may use at most 192 MiB of HBM per device.

v0:
```python
import math
import jax
import jax.numpy as jnp
from jax import lax
from jax.sharding import PartitionSpec as P

HEADS = 12


def layer_norm(values, gain, shift):
    centre = jnp.mean(values, axis=-1, keepdims=True)
    centred = values - centre
    spread = jnp.mean(centred * centred, axis=-1, keepdims=True)
    return centred * lax.rsqrt(spread + 1e-06) * gain + shift


def smooth(values):
    return jax.nn.gelu(values, approximate=True)


def project(inputs, matrix):
    return jnp.einsum("cli,ij->clj", inputs, matrix, preferred_element_type=jnp.float32)


def project_back(grads, matrix):
    return jnp.einsum("clj,ij->cli", grads, matrix, preferred_element_type=jnp.float32)


def outer_sum(inputs, grads):
    return jnp.einsum("cli,clj->ij", inputs, grads, preferred_element_type=jnp.float32)


def token_sum(grads):
    return jnp.sum(grads.astype(jnp.float32), axis=(0, 1))


def masked_scores(query_low, keys_low, keymask, factor):
    raw = (
        jnp.einsum("clhd,cmhd->chlm", query_low, keys_low, preferred_element_type=jnp.float32)
        * factor
    )
    return jnp.where(keymask[:, None, None, :], raw, -1e30)


def per_device(
    hidden,
    lengths,
    cotangent,
    attgain,
    attshift,
    querymat,
    querybias,
    keymat,
    valuemat,
    valuebias,
    mixmat,
    mixbias,
    mlpgain,
    mlpshift,
    upmat_w,
    upbias,
    downmat,
    downbias,
):
    captions, length, width = hidden.shape
    head_size = width // HEADS
    factor = 1.0 / math.sqrt(head_size)
    positions = lax.broadcasted_iota(jnp.int32, (captions, length), 1)
    keymask = positions < lengths[:, None]
    rowmask = keymask.astype(jnp.float32)[..., None]
    gathered = (
        lax.all_gather(attgain, ("dp", "fsdp"), axis=0, tiled=True),
        lax.all_gather(attshift, ("dp", "fsdp"), axis=0, tiled=True),
        lax.all_gather(querymat, ("dp", "fsdp"), axis=1, tiled=True),
        lax.all_gather(querybias, ("dp", "fsdp"), axis=0, tiled=True),
        lax.all_gather(keymat, ("dp", "fsdp"), axis=1, tiled=True),
        lax.all_gather(valuemat, ("dp", "fsdp"), axis=1, tiled=True),
        lax.all_gather(valuebias, ("dp", "fsdp"), axis=0, tiled=True),
        lax.all_gather(mixmat, ("dp", "fsdp"), axis=1, tiled=True),
        lax.all_gather(mixbias, ("dp", "fsdp"), axis=0, tiled=True),
        lax.all_gather(mlpgain, ("dp", "fsdp"), axis=0, tiled=True),
        lax.all_gather(mlpshift, ("dp", "fsdp"), axis=0, tiled=True),
        lax.all_gather(upmat_w, ("dp", "fsdp"), axis=1, tiled=True),
        lax.all_gather(upbias, ("dp", "fsdp"), axis=0, tiled=True),
        lax.all_gather(downmat, ("dp", "fsdp"), axis=1, tiled=True),
        lax.all_gather(downbias, ("dp", "fsdp"), axis=0, tiled=True),
    )
    (
        gain_one,
        shift_one,
        query_w,
        query_b,
        keys_w,
        values_w,
        values_b,
        mixer_w,
        mixer_b,
        gain_two,
        shift_two,
        upper_w,
        upper_b,
        lower_w,
        lower_b,
    ) = gathered
    gain_one = gain_one.astype(jnp.float32)
    shift_one = shift_one.astype(jnp.float32)
    gain_two = gain_two.astype(jnp.float32)
    shift_two = shift_two.astype(jnp.float32)
    source = hidden.astype(jnp.float32)
    normed_low = layer_norm(source, gain_one, shift_one).astype(jnp.bfloat16)
    query_low = (project(normed_low, query_w) + query_b.astype(jnp.float32)).astype(jnp.bfloat16)
    keys_low = project(normed_low, keys_w).astype(jnp.bfloat16)
    values_low = (project(normed_low, values_w) + values_b.astype(jnp.float32)).astype(jnp.bfloat16)
    query_heads = query_low.reshape(captions, length, HEADS, head_size)
    keys_heads = keys_low.reshape(captions, length, HEADS, head_size)
    values_heads = values_low.reshape(captions, length, HEADS, head_size)
    scores = masked_scores(query_heads, keys_heads, keymask, factor)
    peak = jnp.max(scores, axis=-1, keepdims=True)
    logsum = peak + jnp.log(jnp.sum(jnp.exp(scores - peak), axis=-1, keepdims=True))
    probs_low = jnp.exp(scores - logsum).astype(jnp.bfloat16)
    mixed_low = (
        jnp.einsum("chlm,cmhd->clhd", probs_low, values_heads, preferred_element_type=jnp.float32)
        .reshape(captions, length, width)
        .astype(jnp.bfloat16)
    )
    middle = source + project(mixed_low, mixer_w) + mixer_b.astype(jnp.float32)
    normed2_low = layer_norm(middle, gain_two, shift_two).astype(jnp.bfloat16)
    upper = project(normed2_low, upper_w) + upper_b.astype(jnp.float32)
    active_low = smooth(upper).astype(jnp.bfloat16)
    result = middle + project(active_low, lower_w) + lower_b.astype(jnp.float32)
    block_out = result.astype(jnp.bfloat16)
    again = (
        lax.all_gather(attgain, ("dp", "fsdp"), axis=0, tiled=True),
        lax.all_gather(attshift, ("dp", "fsdp"), axis=0, tiled=True),
        lax.all_gather(querymat, ("dp", "fsdp"), axis=1, tiled=True),
        lax.all_gather(querybias, ("dp", "fsdp"), axis=0, tiled=True),
        lax.all_gather(keymat, ("dp", "fsdp"), axis=1, tiled=True),
        lax.all_gather(valuemat, ("dp", "fsdp"), axis=1, tiled=True),
        lax.all_gather(valuebias, ("dp", "fsdp"), axis=0, tiled=True),
        lax.all_gather(mixmat, ("dp", "fsdp"), axis=1, tiled=True),
        lax.all_gather(mixbias, ("dp", "fsdp"), axis=0, tiled=True),
        lax.all_gather(mlpgain, ("dp", "fsdp"), axis=0, tiled=True),
        lax.all_gather(mlpshift, ("dp", "fsdp"), axis=0, tiled=True),
        lax.all_gather(upmat_w, ("dp", "fsdp"), axis=1, tiled=True),
        lax.all_gather(upbias, ("dp", "fsdp"), axis=0, tiled=True),
        lax.all_gather(downmat, ("dp", "fsdp"), axis=1, tiled=True),
        lax.all_gather(downbias, ("dp", "fsdp"), axis=0, tiled=True),
    )
    (
        gain_one,
        shift_one,
        query_w,
        query_b,
        keys_w,
        values_w,
        values_b,
        mixer_w,
        mixer_b,
        gain_two,
        shift_two,
        upper_w,
        upper_b,
        lower_w,
        lower_b,
    ) = again
    gain_one = gain_one.astype(jnp.float32)
    shift_one = shift_one.astype(jnp.float32)
    gain_two = gain_two.astype(jnp.float32)
    shift_two = shift_two.astype(jnp.float32)
    grad_out = cotangent.astype(jnp.float32) * rowmask
    grad_low = grad_out.astype(jnp.bfloat16)
    downmat_grad = outer_sum(active_low, grad_low)
    downbias_grad = token_sum(grad_low)
    grad_active = project_back(grad_low, lower_w)
    gelu_pull = jax.vjp(smooth, upper)[1]
    grad_upper_low = gelu_pull(grad_active)[0].astype(jnp.bfloat16)
    upmat_grad = outer_sum(normed2_low, grad_upper_low)
    upbias_grad = token_sum(grad_upper_low)
    grad_normed2 = project_back(grad_upper_low, upper_w)
    norm_pull = jax.vjp(layer_norm, middle, gain_two, shift_two)[1]
    grad_ln_two, mlpgain_grad, mlpshift_grad = norm_pull(grad_normed2)
    grad_middle = grad_out + grad_ln_two
    mlpgain_grad, mlpshift_grad, upmat_grad, upbias_grad, downmat_grad, downbias_grad = (
        lax.psum_scatter(mlpgain_grad, ("dp", "fsdp"), scatter_dimension=0, tiled=True),
        lax.psum_scatter(mlpshift_grad, ("dp", "fsdp"), scatter_dimension=0, tiled=True),
        lax.psum_scatter(upmat_grad, ("dp", "fsdp"), scatter_dimension=1, tiled=True),
        lax.psum_scatter(upbias_grad, ("dp", "fsdp"), scatter_dimension=0, tiled=True),
        lax.psum_scatter(downmat_grad, ("dp", "fsdp"), scatter_dimension=1, tiled=True),
        lax.psum_scatter(downbias_grad, ("dp", "fsdp"), scatter_dimension=0, tiled=True),
    )
    grad_branch_low = grad_middle.astype(jnp.bfloat16)
    mixmat_grad = outer_sum(mixed_low, grad_branch_low)
    mixbias_grad = token_sum(grad_branch_low)
    grad_mixed_low = (
        project_back(grad_branch_low, mixer_w)
        .astype(jnp.bfloat16)
        .reshape(captions, length, HEADS, head_size)
    )
    scores_again = masked_scores(query_heads, keys_heads, keymask, factor)
    probs = jnp.exp(scores_again - logsum)
    probs_again = probs.astype(jnp.bfloat16)
    grad_values_low = jnp.einsum(
        "chlm,clhd->cmhd", probs_again, grad_mixed_low, preferred_element_type=jnp.float32
    ).astype(jnp.bfloat16)
    grad_probs = jnp.einsum(
        "clhd,cmhd->chlm", grad_mixed_low, values_heads, preferred_element_type=jnp.float32
    )
    weighted = jnp.sum(probs * grad_probs, axis=-1, keepdims=True)
    grad_scores_low = (probs * (grad_probs - weighted)).astype(jnp.bfloat16)
    grad_query_low = (
        jnp.einsum(
            "chlm,cmhd->clhd", grad_scores_low, keys_heads, preferred_element_type=jnp.float32
        )
        * factor
    ).astype(jnp.bfloat16)
    grad_keys_low = (
        jnp.einsum(
            "chlm,clhd->cmhd", grad_scores_low, query_heads, preferred_element_type=jnp.float32
        )
        * factor
    ).astype(jnp.bfloat16)
    grad_query_low = grad_query_low.reshape(captions, length, width)
    grad_keys_low = grad_keys_low.reshape(captions, length, width)
    grad_values_low = grad_values_low.reshape(captions, length, width)
    querymat_grad = outer_sum(normed_low, grad_query_low)
    querybias_grad = token_sum(grad_query_low)
    keymat_grad = outer_sum(normed_low, grad_keys_low)
    valuemat_grad = outer_sum(normed_low, grad_values_low)
    valuebias_grad = token_sum(grad_values_low)
    grad_normed = (
        project_back(grad_query_low, query_w)
        + project_back(grad_keys_low, keys_w)
        + project_back(grad_values_low, values_w)
    )
    first_pull = jax.vjp(layer_norm, source, gain_one, shift_one)[1]
    grad_ln_one, attgain_grad, attshift_grad = first_pull(grad_normed)
    input_grad = grad_middle + grad_ln_one
    (
        attgain_grad,
        attshift_grad,
        querymat_grad,
        querybias_grad,
        keymat_grad,
        valuemat_grad,
        valuebias_grad,
        mixmat_grad,
        mixbias_grad,
    ) = (
        lax.psum_scatter(attgain_grad, ("dp", "fsdp"), scatter_dimension=0, tiled=True),
        lax.psum_scatter(attshift_grad, ("dp", "fsdp"), scatter_dimension=0, tiled=True),
        lax.psum_scatter(querymat_grad, ("dp", "fsdp"), scatter_dimension=1, tiled=True),
        lax.psum_scatter(querybias_grad, ("dp", "fsdp"), scatter_dimension=0, tiled=True),
        lax.psum_scatter(keymat_grad, ("dp", "fsdp"), scatter_dimension=1, tiled=True),
        lax.psum_scatter(valuemat_grad, ("dp", "fsdp"), scatter_dimension=1, tiled=True),
        lax.psum_scatter(valuebias_grad, ("dp", "fsdp"), scatter_dimension=0, tiled=True),
        lax.psum_scatter(mixmat_grad, ("dp", "fsdp"), scatter_dimension=1, tiled=True),
        lax.psum_scatter(mixbias_grad, ("dp", "fsdp"), scatter_dimension=0, tiled=True),
    )
    return (
        block_out,
        input_grad,
        attgain_grad,
        attshift_grad,
        querymat_grad,
        querybias_grad,
        keymat_grad,
        valuemat_grad,
        valuebias_grad,
        mixmat_grad,
        mixbias_grad,
        mlpgain_grad,
        mlpshift_grad,
        upmat_grad,
        upbias_grad,
        downmat_grad,
        downbias_grad,
    )


def solution(mesh):
    placed = (
        P(("dp", "fsdp"), None, None),
        P(("dp", "fsdp")),
        P(("dp", "fsdp"), None, None),
        P(("dp", "fsdp")),
        P(("dp", "fsdp")),
        P(None, ("dp", "fsdp")),
        P(("dp", "fsdp")),
        P(None, ("dp", "fsdp")),
        P(None, ("dp", "fsdp")),
        P(("dp", "fsdp")),
        P(None, ("dp", "fsdp")),
        P(("dp", "fsdp")),
        P(("dp", "fsdp")),
        P(("dp", "fsdp")),
        P(None, ("dp", "fsdp")),
        P(("dp", "fsdp")),
        P(None, ("dp", "fsdp")),
        P(("dp", "fsdp")),
    )
    return jax.shard_map(
        per_device,
        mesh=mesh,
        in_specs=placed,
        out_specs=(
            P(("dp", "fsdp"), None, None),
            P(("dp", "fsdp"), None, None),
            P(("dp", "fsdp")),
            P(("dp", "fsdp")),
            P(None, ("dp", "fsdp")),
            P(("dp", "fsdp")),
            P(None, ("dp", "fsdp")),
            P(None, ("dp", "fsdp")),
            P(("dp", "fsdp")),
            P(None, ("dp", "fsdp")),
            P(("dp", "fsdp")),
            P(("dp", "fsdp")),
            P(("dp", "fsdp")),
            P(None, ("dp", "fsdp")),
            P(("dp", "fsdp")),
            P(None, ("dp", "fsdp")),
            P(("dp", "fsdp")),
        ),
        check_vma=False,
    )
```

profile of v0, /device:TPU:0, one launch (start us, length us, event | category | flops | bytes accessed | tf_op | source)
XLA Modules:
  0.0 1099.5 jit_solution(7005276852524164736)
XLA Ops:
  11.2 0.8 dynamic-update-slice.6
  12.1 0.8 dynamic-update-slice.8
  12.9 0.8 dynamic-update-slice.4
  13.7 0.8 dynamic-update-slice.3
  17.9 0.8 dynamic-update-slice.7
  18.8 42.7 %all-reduce.19 = (bf16[768]{0:T(1024)(128)(2,1)S(1)}, bf16[768]{0:T(1024)(128)(2,1)S(1)}, bf16[768]{0:T(1024)(128)(2,1)S(1)}, bf16[768]{0:T(1024)(128)(2,1)S(1)}...) all-reduce(bf16[768]{0:T(1024)(128)(2,1)S(1)} %dynamic-update-slice, ...), channel_id=1, replica_groups=mesh['dp'=8,'fsdp'=4] {'dp','fsdp'}, use_global_device_ids=true, to_apply=%add.2 | all-reduce | flops 9216 | bytes 36864
  61.5 1.7 convert_reduce_fusion.3
  65.1 2.8 all-gather.9.cloned.1.call-done
  68.0 2.9 add_convert_fusion.2
  70.9 2.7 copy.89
  73.6 50.5 %all-gather.11.cloned.1.call-done = bf16[768,768]{0,1:T(8,128)(2,1)} async-done(((bf16[768,24]{0,1:T(8,128)(2,1)}), bf16[768,768]{0,1:T(8,128)(2,1)}) %all-gather.11.cloned.1.call-update) | async-done | bytes 1179664 | tf_op jit(solution)/shard_map/all_gather | solution.py:76
  124.1 2.9 convolution_convert_fusion.2
  127.0 3.9 reshape.173
  130.9 49.2 %all-gather.7.cloned.1.call-done = bf16[768,768]{0,1:T(8,128)(2,1)} async-done(((bf16[768,24]{0,1:T(8,128)(2,1)}), bf16[768,768]{0,1:T(8,128)(2,1)}) %all-gather.7.cloned.1.call-update) | async-done | bytes 1179664 | tf_op jit(solution)/shard_map/all_gather | solution.py:77
  180.1 2.9 add_convert_fusion.3
  183.0 3.9 reshape.171
  186.9 4.8 fusion.7
  191.7 1.8 exponential_reduce_fusion
  193.5 1.3 copy-done
  194.8 1.3 copy-done.6
  196.1 4.0 convolution_convert_fusion
  200.1 35.8 %all-gather.13.cloned.1.call-done = bf16[768,768]{0,1:T(8,128)(2,1)} async-done(((bf16[768,24]{0,1:T(8,128)(2,1)}), bf16[768,768]{0,1:T(8,128)(2,1)}) %all-gather.13.cloned.1.call-update) | async-done | bytes 1179664 | tf_op jit(solution)/shard_map/all_gather | solution.py:79
  235.9 5.0 fusion.76
  240.9 1.6 copy-done.7
  243.0 58.2 %all-gather.15.cloned.1.call-done = bf16[768,3072]{0,1:T(8,128)(2,1)} async-done(((bf16[768,96]{0,1:T(8,128)(2,1)}), bf16[768,3072]{0,1:T(8,128)(2,1)}) %all-gather.15.cloned.1.call-update) | async-done | bytes 4718608 | tf_op jit(solution)/shard_map/all_gather | solution.py:83
  301.2 11.0 fusion.18
  312.2 54.2 %all-gather.17.cloned.1.call-done = bf16[3072,768]{0,1:T(8,128)(2,1)} async-done(((bf16[3072,24]{0,1:T(8,128)(2,1)}), bf16[3072,768]{0,1:T(8,128)(2,1)}) %all-gather.17.cloned.1.call-update) | async-done | bytes 4718608 | tf_op jit(solution)/shard_map/all_gather | solution.py:85
  366.4 16.4 %convert_reduce_fusion = (f32[3072]{0:T(1024)S(1)}, bf16[16,64,3072]{2,1,0:T(8,128)(2,1)S(1)}) fusion(f32[16,64,3072]{2,1,0:T(8,128)} %fusion.18, f32[3072]{0:T(1024)S(1)} %convert_element_type.143, bf16[3072,768]{0,1:T(8,128)(2,1)} %all-gather.17.cloned.1.call-done, bf16[16,64,768]{2,1,0:T(8,128)(2,1)S(1)} %copy-done.11, f32[16,64]{1,0:T(8,128)S(1)} %get-tuple-element.47), kind=kOutput, calls=%fused_computation.9 | convolution fusion | flops 4906546176 | bytes 25194496 | tf_op jit(solution)/shard_map/clj,ij->cli/dot_general | solution.py:26
  382.8 5.5 multiply_reduce_fusion.1
  388.4 1.3 fusion.75
  390.4 0.9 copy-done.3
  391.4 1.1 copy-done.15
  393.3 4.1 convolution_bitcast_fusion.2
  397.4 4.0 convolution_convert_fusion.1
  401.4 6.2 reshape.174
  407.6 9.3 multiply_reduce_fusion
  416.9 2.6 multiply_convert_fusion.3
  419.5 1.8 fusion.32
  421.3 4.7 copy.79
  425.9 6.2 reshape.176
  432.2 4.7 convolution_bitcast_fusion.4
  437.3 5.0 convert_reduce_fusion.2
  442.3 4.6 copy.75
  447.0 6.1 reshape.175
  453.1 4.7 convolution_bitcast_fusion.5
  458.0 6.6 convert_reduce_fusion.1
  464.5 4.6 copy.81
  469.2 5.2 reshape.177
  474.4 3.2 convolution_bitcast_fusion.3
  477.7 11.0 %convolution_bitcast_fusion.1 = f32[768,3072]{0,1:T(8,128)} fusion(bf16[16,64,3072]{2,1,0:T(8,128)(2,1)} %copy-done.23, f32[16,64,768]{2,1,0:T(8,128)} %copy-done.7, f32[768]{0:T(1024)S(1)} %convert_element_type.141, f32[768]{0:T(1024)S(1)} %convert_element_type.140, f32[16,64]{1,0:T(8,128)S(1)} %fusion.61, f32[16,64]{1,0:T(8,128)S(1)} %broadcast_multiply_fusion), kind=kOutput, calls=%fused_computation.21 | convolution fusion | flops 4835770368 | bytes 18888704 | tf_op jit(solution)/shard_map/cli,clj->ij/dot_general | solution.py:30
  489.0 12.2 %convolution_bitcast_fusion = f32[3072,768]{0,1:T(8,128)} fusion(bf16[16,64,768]{2,1,0:T(8,128)(2,1)} %param.20, f32[16,64]{1,0:T(8,128)S(1)} %get-tuple-element.47, f32[16,64,3072]{2,1,0:T(8,128)} %fusion.18, f32[3072]{0:T(1024)S(1)} %convert_element_type.143), kind=kOutput, calls=%fused_computation.20 | convolution fusion | flops 4865654784 | bytes 23609344 | tf_op jit(solution)/shard_map/cli,clj->ij/dot_general | solution.py:30
  502.0 3.3 fusion.50
  505.3 1.4 fusion.53
  506.7 1.9 fusion.73
  508.7 1.6 copy-done.5
  510.4 1.7 fusion.27
  512.0 40.8 %all-reduce.18 = (f32[768]{0:T(1024)S(1)}, f32[768]{0:T(1024)S(1)}, f32[768]{0:T(1024)S(1)}, f32[768]{0:T(1024)S(1)}, f32[768]{0:T(1024)S(1)}, /*index=5*/f32[76...) all-reduce(f32[768]{0:T(1024)S(1)} %get-tuple-element.19, ...), channel_id=2, replica_groups=mesh['dp'=8,'fsdp'=4] {'dp','fsdp'}, use_global_device_ids=true, to_apply=%region_12.13.clone | all-reduce | flops 9216 | bytes 73728
  558.1 5.0 add_add_fusion.2
  563.1 13.2 %add_convert_fusion = bf16[16,64,768]{2,1,0:T(8,128)(2,1)} fusion(f32[16,64,768]{2,1,0:T(8,128)S(1)} %copy-done.9, bf16[3072,768]{0,1:T(8,128)(2,1)} %all-gather.17.cloned.1.call-done, f32[768]{0:T(1024)S(1)} %convert_element_type.145, f32[16,64,3072]{2,1,0:T(8,128)} %fusion.18, f32[3072]{0:T(1024)S(1)} %convert_element_type.143), kind=kOutput, calls=%fused_computation.61 | convolution fusion | flops 4865654784 | bytes 22035456 | tf_op jit(solution)/shard_map/cli,ij->clj/dot_general | solution.py:22
  576.3 24.0 %reduce-scatter.9.cloned.1.call-done = f32[768,24]{0,1:T(8,128)} async-done(((f32[768,768]{0,1:T(8,128)}), f32[768,24]{0,1:T(8,128)}) %reduce-scatter.9.cloned.1.call-update) | async-done | bytes 73744 | tf_op jit(solution)/shard_map/reduce_scatter | solution.py:253
  600.4 103.9 %reduce-scatter.7.cloned.1.call-done = f32[768,24]{0,1:T(8,128)} async-done(((f32[768,768]{0,1:T(8,128)}), f32[768,24]{0,1:T(8,128)}) %reduce-scatter.7.cloned.1.call-update) | async-done | bytes 73744 | tf_op jit(solution)/shard_map/reduce_scatter | solution.py:251
  704.3 104.7 %reduce-scatter.11.cloned.1.call-done = f32[768,24]{0,1:T(8,128)} async-done(((f32[768,768]{0,1:T(8,128)}), f32[768,24]{0,1:T(8,128)}) %reduce-scatter.11.cloned.1.call-update) | async-done | bytes 73744 | tf_op jit(solution)/shard_map/reduce_scatter | solution.py:254
  809.0 141.2 %reduce-scatter.15.cloned.1.call-done = f32[768,96]{0,1:T(8,128)} async-done(((f32[768,3072]{0,1:T(8,128)}), f32[768,96]{0,1:T(8,128)}) %reduce-scatter.15.cloned.1.call-update) | async-done | bytes 294928 | tf_op jit(solution)/shard_map/reduce_scatter | solution.py:186
  950.2 142.0 %reduce-scatter.17.cloned.1.call-done = f32[3072,24]{0,1:T(8,128)} async-done(((f32[3072,768]{0,1:T(8,128)}), f32[3072,24]{0,1:T(8,128)}) %reduce-scatter.17.cloned.1.call-update) | async-done | bytes 294928 | tf_op jit(solution)/shard_map/reduce_scatter | solution.py:188
  (118 shorter events, 18.4 us)
Async XLA Ops:
  7.2 56.8 %copy-start.1 = (bf16[16,64,768]{2,1,0:T(8,128)(2,1)S(1)}, bf16[16,64,768]{2,1,0:T(8,128)(2,1)}, u32[]{:S(2)}) copy-start(bf16[16,64,768]{2,1,0:T(8,128)(2,1)} %param.18) | copy-start | bytes 4718596
  7.2 60.8 %all-gather.9.cloned.1.call-start = ((), (), s32[]{:S(2)}) async-start(), calls=%async_computation.7 | async-start | bytes 1216512 | tf_op jit(solution)/shard_map/all_gather | solution.py:74
  7.9 116.2 %all-gather.11.cloned.1.call-start = ((), (), s32[]{:S(2)}) async-start(), calls=%async_computation.8 | async-start | bytes 1216512 | tf_op jit(solution)/shard_map/all_gather | solution.py:76
  8.7 171.4 %all-gather.7.cloned.1.call-start = ((), (), s32[]{:S(2)}) async-start(), calls=%async_computation.6 | async-start | bytes 1216512 | tf_op jit(solution)/shard_map/all_gather | solution.py:77
  9.4 226.5 %all-gather.13.cloned.1.call-start = ((), (), s32[]{:S(2)}) async-start(), calls=%async_computation.9 | async-start | bytes 1216512 | tf_op jit(solution)/shard_map/all_gather | solution.py:79
  10.0 291.2 %all-gather.15.cloned.1.call-start = ((), (), s32[]{:S(2)}) async-start(), calls=%async_computation.10 | async-start | bytes 4866048 | tf_op jit(solution)/shard_map/all_gather | solution.py:83
  10.6 355.8 %all-gather.17.cloned.1.call-start = ((), (), s32[]{:S(2)}) async-start(), calls=%async_computation.11 | async-start | bytes 4866048 | tf_op jit(solution)/shard_map/all_gather | solution.py:85
  11.2 565.2 %reduce-scatter.13.cloned.1.call-start = ((), (), s32[]{:S(2)}) async-start(), calls=%async_computation.15 | async-start | bytes 2433024 | tf_op jit(solution)/shard_map/reduce_scatter | solution.py:256
  64.5 0.6 copy-start.17
  191.6 3.2 copy-start
  191.7 4.5 copy-start.6
  240.9 1.6 copy-start.7
  243.0 123.4 %copy-start.11 = (bf16[16,64,768]{2,1,0:T(8,128)(2,1)S(1)}, bf16[16,64,768]{2,1,0:T(8,128)(2,1)}, u32[]{:S(2)}) copy-start(bf16[16,64,768]{2,1,0:T(8,128)(2,1)} %param.20) | copy-start | bytes 4718596
  366.4 16.4 %copy-start.8 = (f32[16,64,768]{2,1,0:T(8,128)S(1)}, f32[16,64,768]{2,1,0:T(8,128)}, u32[]{:S(2)}) copy-start(f32[16,64,768]{2,1,0:T(8,128)} %copy-done.7) | copy-start | bytes 9437188
  366.4 16.4 %copy-start.20 = (bf16[768,3072]{0,1:T(8,128)(2,1)S(1)}, bf16[768,3072]{0,1:T(8,128)(2,1)}, u32[]{:S(2)}) copy-start(bf16[768,3072]{0,1:T(8,128)(2,1)} %all-gather.15.cloned.1.call-done) | copy-start | bytes 14155780
  382.8 5.6 copy-start.23
  389.7 1.7 copy-start.3
  389.7 3.6 copy-start.13
  391.4 1.1 copy-start.15
  393.3 4.1 copy-start.22
  397.3 203.0 %reduce-scatter.9.cloned.1.call-start = ((), (), s32[]{:S(2)}) async-start(), calls=%async_computation.13 | async-start | bytes 2433024 | tf_op jit(solution)/shard_map/reduce_scatter | solution.py:253
  401.4 15.5 %slice-start = ((s8[6291456]{0:T(1024)(128)(4,1)}), s8[2097152]{0:T(1024)(128)(4,1)S(1)}, s32[]{:S(2)}) async-start(s8[6291456]{0:T(1024)(128)(4,1)} %bitcast.80), calls=%async_computation.18 | async-start | bytes 4194304
  407.6 9.3 slice-start.1
  416.9 2.6 copy-start.4
  419.5 1.8 copy-start.10
  425.9 6.2 copy-start.2
  436.9 267.4 %reduce-scatter.7.cloned.1.call-start = ((), (), s32[]{:S(2)}) async-start(), calls=%async_computation.12 | async-start | bytes 2433024 | tf_op jit(solution)/shard_map/reduce_scatter | solution.py:251
  457.8 351.2 %reduce-scatter.11.cloned.1.call-start = ((), (), s32[]{:S(2)}) async-start(), calls=%async_computation.14 | async-start | bytes 2433024 | tf_op jit(solution)/shard_map/reduce_scatter | solution.py:254
  477.6 472.6 %reduce-scatter.15.cloned.1.call-start = ((), (), s32[]{:S(2)}) async-start(), calls=%async_computation.16 | async-start | bytes 9732096 | tf_op jit(solution)/shard_map/reduce_scatter | solution.py:186
  488.7 603.5 %reduce-scatter.17.cloned.1.call-start = ((), (), s32[]{:S(2)}) async-start(), calls=%async_computation.17 | async-start | bytes 9732096 | tf_op jit(solution)/shard_map/reduce_scatter | solution.py:188
  501.2 0.7 copy-start.19
  502.0 3.3 copy-start.14
  502.0 3.3 copy-start.21
  505.3 1.4 copy-start.16
  506.7 2.0 copy-start.18
  508.7 1.7 copy-start.5
  508.7 49.4 %copy-start.12 = (bf16[16,64,768]{2,1,0:T(8,128)(2,1)S(1)}, bf16[16,64,768]{2,1,0:T(8,128)(2,1)}, u32[]{:S(2)}) copy-start(bf16[16,64,768]{2,1,0:T(8,128)(2,1)} %param.20) | copy-start | bytes 4718596
  558.1 5.0 copy-start.9
Sparse Core Ops, SparseCore 0:
  10.9 56.9 all-gather.8
  70.9 53.1 all-gather.10
  127.0 53.0 all-gather.6
  182.8 53.0 all-gather.12
  238.6 62.5 all-gather.14
  304.0 62.3 all-gather.16
  397.5 97.8 reduce-scatter.12
  502.1 98.2 reduce-scatter.8
  606.2 98.0 reduce-scatter.6
  710.8 98.0 reduce-scatter.10
  815.5 134.6 reduce-scatter.14
  957.5 134.6 reduce-scatter.16
where the time goes:
time: 1110 us; the launch traced here: 1100 us
  waiting for transfers between devices  770 us (69%)
  matrix products  142 us (13%)
  blocking collectives  83.5 us (8%)
  local copies, waits for them, and re-layouts  71 us (6%)
  other arithmetic  16.6 us (1%)
  between operations  15.2 us (1%)
    reduce_scatter x1, waiting for transfers between devices, per_device(): lax.psum_scatter(downmat_grad, ('dp', 'fsdp'), scatter_dimension=1, tiled...  142 us
    reduce_scatter x1, waiting for transfers between devices, per_device(): lax.psum_scatter(upmat_grad, ('dp', 'fsdp'), scatter_dimension=1, tiled=T...  141 us
    reduce_scatter x1, waiting for transfers between devices, per_device(): lax.psum_scatter(valuemat_grad, ('dp', 'fsdp'), scatter_dimension=1, tile...  105 us
    reduce_scatter x1, waiting for transfers between devices, per_device(): lax.psum_scatter(querymat_grad, ('dp', 'fsdp'), scatter_dimension=1, tile...  104 us
    unnamed x2, blocking collectives  83.5 us
    all_gather x1, waiting for transfers between devices, per_device(): lax.all_gather(upmat_w, ('dp', 'fsdp'), axis=1, tiled=True)  58.2 us
    all_gather x1, waiting for transfers between devices, per_device(): lax.all_gather(downmat, ('dp', 'fsdp'), axis=1, tiled=True)  54.2 us
    all_gather x1, waiting for transfers between devices, per_device(): lax.all_gather(keymat, ('dp', 'fsdp'), axis=1, tiled=True)  50.5 us
  transfers between devices with their start and end apart: 12, of which 11 were waited for; matrix products, arithmetic and copies ran while one was open for 17% of the time, Pallas kernels for 0%

commit v1 on v0

--- a/solution.py
+++ b/solution.py
@@ -5,6 +5,18 @@
 from jax.sharding import PartitionSpec as P
 
 HEADS = 12
+
+
+def gather_by_bits(x, axis, dim):
+    ways, here = (lax.axis_size(axis), lax.axis_index(axis))
+    grown, reach = (x, 1)
+    while reach < ways:
+        theirs = lax.ppermute(grown, axis, [(d, d ^ reach) for d in range(ways)])
+        mine_first = jnp.concatenate([grown, theirs], axis=dim)
+        theirs_first = jnp.concatenate([theirs, grown], axis=dim)
+        grown = jnp.where(here & reach == 0, mine_first, theirs_first)
+        reach = 2 * reach
+    return grown
 
 
 def layer_norm(values, gain, shift):
@@ -82,7 +94,7 @@
         lax.all_gather(mlpshift, ("dp", "fsdp"), axis=0, tiled=True),
         lax.all_gather(upmat_w, ("dp", "fsdp"), axis=1, tiled=True),
         lax.all_gather(upbias, ("dp", "fsdp"), axis=0, tiled=True),
-        lax.all_gather(downmat, ("dp", "fsdp"), axis=1, tiled=True),
+        gather_by_bits(downmat, ("dp", "fsdp"), 1),
         lax.all_gather(downbias, ("dp", "fsdp"), axis=0, tiled=True),
     )
     (

time: 1110 us -> 1220 us (1.099)
  blocking collectives: 83.5 us -> 156 us
  waiting for transfers between devices: 770 us -> 786 us
    reduce_scatter x1, waiting for transfers between devices: 104 us -> 0.01 us  [per_device(): lax.psum_scatter(querymat_grad, ('dp', 'fsdp'), scatter_dimension=1, tile...]
    reduce_scatter x1, waiting for transfers between devices: 0.01 us -> 96.6 us  [per_device(): lax.psum_scatter(mixmat_grad, ('dp', 'fsdp'), scatter_dimension=1, tiled=...]
    unnamed x2, blocking collectives: 83.5 us -> 156 us
    ppermute x0 -> x5, waiting for transfers between devices: none -> 47.5 us  [gather_by_bits(): theirs = lax.ppermute(grown, axis, [(d, d ^ reach) for d in range(ways)])]
    reduce_scatter x1, waiting for transfers between devices: 24 us -> 0.01 us  [per_device(): lax.psum_scatter(keymat_grad, ('dp', 'fsdp'), scatter_dimension=1, tiled=...]
  transfers between devices with their start and end apart: 12 -> 17, of which waited for: 11 -> 14; matrix products, arithmetic and copies ran while one was open for 17% -> 14% of each run, Pallas kernels for 0% -> 0%
where the time goes in v1:
time: 1220 us; the launch traced here: 1210 us
  waiting for transfers between devices  786 us (64%)
  blocking collectives  156 us (13%)
  matrix products  147 us (12%)
  local copies, waits for them, and re-layouts  70.7 us (6%)
  other arithmetic  26.9 us (2%)
  between operations  15.1 us (1%)
    unnamed x2, blocking collectives  156 us
    reduce_scatter x1, waiting for transfers between devices, per_device(): lax.psum_scatter(downmat_grad, ('dp', 'fsdp'), scatter_dimension=1, tiled...  142 us
    reduce_scatter x1, waiting for transfers between devices, per_device(): lax.psum_scatter(upmat_grad, ('dp', 'fsdp'), scatter_dimension=1, tiled=T...  141 us
    reduce_scatter x1, waiting for transfers between devices, per_device(): lax.psum_scatter(valuemat_grad, ('dp', 'fsdp'), scatter_dimension=1, tile...  105 us
    reduce_scatter x1, waiting for transfers between devices, per_device(): lax.psum_scatter(mixmat_grad, ('dp', 'fsdp'), scatter_dimension=1, tiled=...  96.6 us
    all_gather x1, waiting for transfers between devices, per_device(): lax.all_gather(upmat_w, ('dp', 'fsdp'), axis=1, tiled=True)  58.2 us
    all_gather x1, waiting for transfers between devices, per_device(): lax.all_gather(downmat, ('dp', 'fsdp'), axis=1, tiled=True)  54.3 us
    all_gather x1, waiting for transfers between devices, per_device(): lax.all_gather(keymat, ('dp', 'fsdp'), axis=1, tiled=True)  50.5 us
  transfers between devices with their start and end apart: 17, of which 14 were waited for; matrix products, arithmetic and copies ran while one was open for 14% of the time, Pallas kernels for 0%

profile of v1, /device:TPU:0, one launch (start us, length us, event | category | flops | bytes accessed | tf_op | source)
XLA Modules:
  0.0 1210.0 jit_solution(15888384189764160991)
XLA Ops:
  18.8 42.7 %all-reduce.19 = (bf16[768]{0:T(1024)(128)(2,1)S(1)}, bf16[768]{0:T(1024)(128)(2,1)S(1)}, bf16[768]{0:T(1024)(128)(2,1)S(1)}, bf16[768]{0:T(1024)(128)(2,1)S(1)}...) all-reduce(bf16[768]{0:T(1024)(128)(2,1)S(1)} %dynamic-update-slice, ...), channel_id=1, replica_groups=mesh['dp'=8,'fsdp'=4] {'dp','fsdp'}, use_global_device_ids=true, to_apply=%add.2 | all-reduce | flops 9216 | bytes 36864
  61.5 1.7 convert_reduce_fusion.3
  65.1 2.8 all-gather.9.cloned.1.call-done
  68.0 2.9 add_convert_fusion.2
  70.9 2.7 copy.94
  73.6 50.5 %all-gather.11.cloned.1.call-done = bf16[768,768]{0,1:T(8,128)(2,1)} async-done(((bf16[768,24]{0,1:T(8,128)(2,1)}), bf16[768,768]{0,1:T(8,128)(2,1)}) %all-gather.11.cloned.1.call-update) | async-done | bytes 1179664 | tf_op jit(solution)/shard_map/all_gather | solution.py:88
  124.1 2.9 convolution_convert_fusion.2
  127.0 3.9 reshape.173
  130.9 49.1 %all-gather.7.cloned.1.call-done = bf16[768,768]{0,1:T(8,128)(2,1)} async-done(((bf16[768,24]{0,1:T(8,128)(2,1)}), bf16[768,768]{0,1:T(8,128)(2,1)}) %all-gather.7.cloned.1.call-update) | async-done | bytes 1179664 | tf_op jit(solution)/shard_map/all_gather | solution.py:89
  180.1 2.9 add_convert_fusion.3
  183.0 3.9 reshape.171
  186.9 4.8 fusion.7
  191.7 1.8 exponential_reduce_fusion
  193.5 1.3 copy-done
  196.1 3.6 convolution_convert_fusion
  199.8 36.1 %all-gather.13.cloned.1.call-done = bf16[768,768]{0,1:T(8,128)(2,1)} async-done(((bf16[768,24]{0,1:T(8,128)(2,1)}), bf16[768,768]{0,1:T(8,128)(2,1)}) %all-gather.13.cloned.1.call-update) | async-done | bytes 1179664 | tf_op jit(solution)/shard_map/all_gather | solution.py:91
  235.9 5.0 fusion.84
  240.9 1.6 copy-done.7
  243.0 58.2 %all-gather.15.cloned.1.call-done = bf16[768,3072]{0,1:T(8,128)(2,1)} async-done(((bf16[768,96]{0,1:T(8,128)(2,1)}), bf16[768,3072]{0,1:T(8,128)(2,1)}) %all-gather.15.cloned.1.call-update) | async-done | bytes 4718608 | tf_op jit(solution)/shard_map/all_gather | solution.py:95
  301.2 10.9 fusion.24
  312.1 54.3 %all-gather.17.cloned.1.call-done = bf16[3072,768]{0,1:T(8,128)(2,1)} async-done(((bf16[3072,24]{0,1:T(8,128)(2,1)}), bf16[3072,768]{0,1:T(8,128)(2,1)}) %all-gather.17.cloned.1.call-update) | async-done | bytes 4718608 | tf_op jit(solution)/shard_map/all_gather | solution.py:158
  366.4 16.4 %convert_reduce_fusion = (f32[3072]{0:T(1024)S(1)}, bf16[16,64,3072]{2,1,0:T(8,128)(2,1)S(1)}) fusion(f32[16,64,3072]{2,1,0:T(8,128)} %fusion.24, f32[3072]{0:T(1024)S(1)} %convert_element_type.143, bf16[3072,768]{0,1:T(8,128)(2,1)} %all-gather.17.cloned.1.call-done, bf16[16,64,768]{2,1,0:T(8,128)(2,1)S(1)} %copy-done.11, f32[16,64]{1,0:T(8,128)S(1)} %get-tuple-element.47), kind=kOutput, calls=%fused_computation.9 | convolution fusion | flops 4906546176 | bytes 25194496 | tf_op jit(solution)/shard_map/clj,ij->cli/dot_general | solution.py:38
  382.8 5.5 multiply_reduce_fusion.1
  392.6 2.5 convolution_convert_fusion.1
  395.1 6.0 reshape.174
  401.1 9.1 multiply_reduce_fusion
  410.2 3.0 multiply_convert_fusion.3
  413.2 1.8 fusion.39
  415.0 4.6 copy.82
  419.6 6.2 reshape.176
  425.8 4.6 convolution_bitcast_fusion.4
  430.5 5.0 convert_reduce_fusion.2
  435.5 4.7 copy.78
  440.2 6.3 reshape.175
  446.4 4.7 convolution_bitcast_fusion.5
  451.2 6.5 convolution_bitcast_fusion.2
  457.7 6.7 convert_reduce_fusion.1
  464.4 4.6 copy.84
  469.0 5.4 reshape.177
  474.4 3.1 convolution_bitcast_fusion.3
  477.6 11.1 convolution_bitcast_fusion.1
  488.8 12.2 %convolution_bitcast_fusion = f32[3072,768]{0,1:T(8,128)} fusion(bf16[16,64,768]{2,1,0:T(8,128)(2,1)} %param.20, f32[16,64]{1,0:T(8,128)S(1)} %get-tuple-element.47, f32[16,64,3072]{2,1,0:T(8,128)} %fusion.24, f32[3072]{0:T(1024)S(1)} %convert_element_type.143), kind=kOutput, calls=%fused_computation.20 | convolution fusion | flops 4865654784 | bytes 23609344 | tf_op jit(solution)/shard_map/cli,clj->ij/dot_general | solution.py:42
  504.6 1.6 collective-permute-start.1
  506.2 7.7 collective-permute-done.1
  514.0 2.0 maximum_select_fusion.3
  516.0 1.5 collective-permute-start.2
  517.5 13.6 %collective-permute-done.2 = bf16[3072,96]{0,1:T(8,128)(2,1)} collective-permute-done((bf16[3072,96]{0,1:T(8,128)(2,1)}, bf16[3072,96]{0,1:T(8,128)(2,1)}, u32[]{:S(2)}, u32[]{:S(2)}) %collective-permute-start.2) | collective-permute-done | bytes 589856 | tf_op jit(solution)/shard_map/ppermute | solution.py:14
  531.0 3.1 maximum_select_fusion.2
  534.1 1.9 collective-permute-start.3
  536.0 25.0 %collective-permute-done.3 = bf16[3072,192]{0,1:T(8,128)(2,1)} collective-permute-done((bf16[3072,192]{0,1:T(8,128)(2,1)}, bf16[3072,192]{0,1:T(8,128)(2,1)}, u32[]{:S(2)}, u32[]{:S(2)}) %collective-permute-start.3) | collective-permute-done | bytes 1179680 | tf_op jit(solution)/shard_map/ppermute | solution.py:14
  560.9 3.7 maximum_select_fusion.1
  564.6 2.4 collective-permute-start.4
  567.0 3.1 fusion.57
  570.1 3.1 fusion.60
  573.3 5.0 fusion.81
  578.4 1.6 copy-done.5
  580.0 1.7 fusion.34
  581.7 113.2 %all-reduce.18 = (f32[768]{0:T(1024)S(1)}, f32[768]{0:T(1024)S(1)}, f32[768]{0:T(1024)S(1)}, f32[768]{0:T(1024)S(1)}, f32[768]{0:T(1024)S(1)}, /*index=5*/f32[76...) all-reduce(f32[768]{0:T(1024)S(1)} %get-tuple-element.19, ...), channel_id=2, replica_groups=mesh['dp'=8,'fsdp'=4] {'dp','fsdp'}, use_global_device_ids=true, to_apply=%region_12.13.clone | all-reduce | flops 9216 | bytes 73728
  700.1 4.9 add_add_fusion.2
  705.0 13.5 %add_convert_fusion = bf16[16,64,768]{2,1,0:T(8,128)(2,1)} fusion(f32[16,64,768]{2,1,0:T(8,128)S(1)} %copy-done.9, bf16[3072,384]{0,1:T(8,128)(2,1)} %collective-permute-done.4, bf16[3072,384]{0,1:T(8,128)(2,1)} %maximum_select_fusion.1, pred[]{:T(512)S(6)} %eq.15, f32[768]{0:T(1024)S(1)} %convert_element_type.145, f32[16,64,3072]{2,1,0:T(8,128)} %fusion.24, ...), kind=kOutput, calls=%fused_computation.68 | convolution fusion | flops 4886888448 | bytes 22035456 | tf_op jit(solution)/shard_map/cli,ij->clj/dot_general | solution.py:34
  718.6 96.6 %reduce-scatter.13.cloned.1.call-done = f32[768,24]{0,1:T(8,128)} async-done(((f32[768,768]{0,1:T(8,128)}), f32[768,24]{0,1:T(8,128)}) %reduce-scatter.13.cloned.1.call-update) | async-done | bytes 73744 | tf_op jit(solution)/shard_map/reduce_scatter | solution.py:268
  815.2 104.6 %reduce-scatter.11.cloned.1.call-done = f32[768,24]{0,1:T(8,128)} async-done(((f32[768,768]{0,1:T(8,128)}), f32[768,24]{0,1:T(8,128)}) %reduce-scatter.11.cloned.1.call-update) | async-done | bytes 73744 | tf_op jit(solution)/shard_map/reduce_scatter | solution.py:266
  919.8 141.0 %reduce-scatter.15.cloned.1.call-done = f32[768,96]{0,1:T(8,128)} async-done(((f32[768,3072]{0,1:T(8,128)}), f32[768,96]{0,1:T(8,128)}) %reduce-scatter.15.cloned.1.call-update) | async-done | bytes 294928 | tf_op jit(solution)/shard_map/reduce_scatter | solution.py:198
  1060.8 142.0 %reduce-scatter.17.cloned.1.call-done = f32[3072,24]{0,1:T(8,128)} async-done(((f32[3072,768]{0,1:T(8,128)}), f32[3072,24]{0,1:T(8,128)}) %reduce-scatter.17.cloned.1.call-update) | async-done | bytes 294928 | tf_op jit(solution)/shard_map/reduce_scatter | solution.py:200
  (134 shorter events, 28.6 us)
Async XLA Ops:
  7.2 56.8 %copy-start.1 = (bf16[16,64,768]{2,1,0:T(8,128)(2,1)S(1)}, bf16[16,64,768]{2,1,0:T(8,128)(2,1)}, u32[]{:S(2)}) copy-start(bf16[16,64,768]{2,1,0:T(8,128)(2,1)} %param.18) | copy-start | bytes 4718596
  7.2 60.8 %all-gather.9.cloned.1.call-start = ((), (), s32[]{:S(2)}) async-start(), calls=%async_computation.7 | async-start | bytes 1216512 | tf_op jit(solution)/shard_map/all_gather | solution.py:86
  7.9 116.2 %all-gather.11.cloned.1.call-start = ((), (), s32[]{:S(2)}) async-start(), calls=%async_computation.8 | async-start | bytes 1216512 | tf_op jit(solution)/shard_map/all_gather | solution.py:88
  8.7 171.4 %all-gather.7.cloned.1.call-start = ((), (), s32[]{:S(2)}) async-start(), calls=%async_computation.6 | async-start | bytes 1216512 | tf_op jit(solution)/shard_map/all_gather | solution.py:89
  9.4 226.5 %all-gather.13.cloned.1.call-start = ((), (), s32[]{:S(2)}) async-start(), calls=%async_computation.9 | async-start | bytes 1216512 | tf_op jit(solution)/shard_map/all_gather | solution.py:91
  10.0 291.2 %all-gather.15.cloned.1.call-start = ((), (), s32[]{:S(2)}) async-start(), calls=%async_computation.10 | async-start | bytes 4866048 | tf_op jit(solution)/shard_map/all_gather | solution.py:95
  10.6 355.8 %all-gather.17.cloned.1.call-start = ((), (), s32[]{:S(2)}) async-start(), calls=%async_computation.11 | async-start | bytes 4866048 | tf_op jit(solution)/shard_map/all_gather | solution.py:158
  11.2 707.4 %reduce-scatter.9.cloned.1.call-start = ((), (), s32[]{:S(2)}) async-start(), calls=%async_computation.13 | async-start | bytes 2433024 | tf_op jit(solution)/shard_map/reduce_scatter | solution.py:265
  64.5 0.6 copy-start.17
  191.7 3.2 copy-start
  191.7 4.5 copy-start.6
  240.9 1.6 copy-start.7
  243.0 123.4 %copy-start.11 = (bf16[16,64,768]{2,1,0:T(8,128)(2,1)S(1)}, bf16[16,64,768]{2,1,0:T(8,128)(2,1)}, u32[]{:S(2)}) copy-start(bf16[16,64,768]{2,1,0:T(8,128)(2,1)} %param.20) | copy-start | bytes 4718596
  366.4 16.4 %copy-start.8 = (f32[16,64,768]{2,1,0:T(8,128)S(1)}, f32[16,64,768]{2,1,0:T(8,128)}, u32[]{:S(2)}) copy-start(f32[16,64,768]{2,1,0:T(8,128)} %copy-done.7) | copy-start | bytes 9437188
  366.4 16.4 %copy-start.20 = (bf16[768,3072]{0,1:T(8,128)(2,1)S(1)}, bf16[768,3072]{0,1:T(8,128)(2,1)}, u32[]{:S(2)}) copy-start(bf16[768,3072]{0,1:T(8,128)(2,1)} %all-gather.15.cloned.1.call-done) | copy-start | bytes 14155780
  382.8 5.6 copy-start.24
  389.7 1.7 copy-start.3
  389.7 2.9 copy-start.23
  391.4 1.1 copy-start.15
  395.1 15.1 %slice-start = ((s8[6291456]{0:T(1024)(128)(4,1)}), s8[2097152]{0:T(1024)(128)(4,1)S(1)}, s32[]{:S(2)}) async-start(s8[6291456]{0:T(1024)(128)(4,1)} %bitcast.81), calls=%async_computation.18 | async-start | bytes 4194304
  401.1 9.1 slice-start.1
  410.2 3.0 copy-start.4
  413.2 1.8 copy-start.10
  419.6 6.2 copy-start.2
  430.4 288.1 %reduce-scatter.7.cloned.1.call-start = ((), (), s32[]{:S(2)}) async-start(), calls=%async_computation.12 | async-start | bytes 2433024 | tf_op jit(solution)/shard_map/reduce_scatter | solution.py:263
  451.1 364.1 %reduce-scatter.13.cloned.1.call-start = ((), (), s32[]{:S(2)}) async-start(), calls=%async_computation.15 | async-start | bytes 2433024 | tf_op jit(solution)/shard_map/reduce_scatter | solution.py:268
  457.7 462.1 %reduce-scatter.11.cloned.1.call-start = ((), (), s32[]{:S(2)}) async-start(), calls=%async_computation.14 | async-start | bytes 2433024 | tf_op jit(solution)/shard_map/reduce_scatter | solution.py:266
  477.6 583.2 %reduce-scatter.15.cloned.1.call-start = ((), (), s32[]{:S(2)}) async-start(), calls=%async_computation.16 | async-start | bytes 9732096 | tf_op jit(solution)/shard_map/reduce_scatter | solution.py:198
  488.8 714.0 %reduce-scatter.17.cloned.1.call-start = ((), (), s32[]{:S(2)}) async-start(), calls=%async_computation.17 | async-start | bytes 9732096 | tf_op jit(solution)/shard_map/reduce_scatter | solution.py:200
  501.0 0.9 copy-start.16
  501.9 34.0 %copy-start.19 = (bf16[768]{0:T(1024)(128)(2,1)S(1)}, bf16[768]{0:T(1024)(128)(2,1)}, u32[]{:S(2)}) copy-start(bf16[768]{0:T(1024)(128)(2,1)} %get-tuple-element.38) | copy-start | bytes 4612
  501.9 1.5 collective-permute-start
  504.6 9.3 collective-permute-start.1
  516.0 15.0 %collective-permute-start.2 = (bf16[3072,96]{0,1:T(8,128)(2,1)}, bf16[3072,96]{0,1:T(8,128)(2,1)}, u32[]{:S(2)}, u32[]{:S(2)}) collective-permute-start(bf16[3072,96]{0,1:T(8,128)(2,1)} %maximum_select_fusion.3), channel_id=1, source_target_pairs={{0,4},{1,5},{2,6},{3,7},{4,0},{5,1},{6,2},{7,3},{8,12},{9,13},{10,... | collective-permute-start | bytes 1769480 | tf_op jit(solution)/shard_map/ppermute | solution.py:14
  534.1 26.8 %collective-permute-start.3 = (bf16[3072,192]{0,1:T(8,128)(2,1)}, bf16[3072,192]{0,1:T(8,128)(2,1)}, u32[]{:S(2)}, u32[]{:S(2)}) collective-permute-start(bf16[3072,192]{0,1:T(8,128)(2,1)} %maximum_select_fusion.2), channel_id=1, source_target_pairs={{0,8},{1,9},{2,10},{3,11},{4,12},{5,13},{6,14},{7,15},{8,0},{9,1},... | collective-permute-start | bytes 3538952 | tf_op jit(solution)/shard_map/ppermute | solution.py:14
  535.9 31.1 %copy-start.13 = (bf16[16,64,768]{2,1,0:T(8,128)(2,1)S(1)}, bf16[16,64,768]{2,1,0:T(8,128)(2,1)}, u32[]{:S(2)}) copy-start(bf16[16,64,768]{2,1,0:T(8,128)(2,1)} %reshape.176) | copy-start | bytes 4718596
  536.0 31.1 %copy-start.22 = (bf16[768,768]{0,1:T(8,128)(2,1)S(1)}, bf16[768,768]{0,1:T(8,128)(2,1)}, u32[]{:S(2)}) copy-start(bf16[768,768]{0,1:T(8,128)(2,1)} %all-gather.11.cloned.1.call-done) | copy-start | bytes 3538948
  564.6 5.4 copy-start.14
  564.6 5.4 copy-start.21
  564.6 140.4 %collective-permute-start.4 = (bf16[3072,384]{0,1:T(8,128)(2,1)}, bf16[3072,384]{0,1:T(8,128)(2,1)}, u32[]{:S(2)}, u32[]{:S(2)}) collective-permute-start(bf16[3072,384]{0,1:T(8,128)(2,1)} %maximum_select_fusion.1), channel_id=1, source_target_pairs={{0,16},{1,17},{2,18},{3,19},{4,20},{5,21},{6,22},{7,23},{8,24},{9,... | collective-permute-start | bytes 7077896 | tf_op jit(solution)/shard_map/ppermute | solution.py:14
  573.3 5.1 copy-start.18
  578.3 1.7 copy-start.5
  578.3 121.8 %copy-start.12 = (bf16[16,64,768]{2,1,0:T(8,128)(2,1)S(1)}, bf16[16,64,768]{2,1,0:T(8,128)(2,1)}, u32[]{:S(2)}) copy-start(bf16[16,64,768]{2,1,0:T(8,128)(2,1)} %param.20) | copy-start | bytes 4718596
  700.1 4.9 copy-start.9
Sparse Core Ops, SparseCore 0:
  10.9 56.9 all-gather.8
  70.9 53.1 all-gather.10
  127.0 53.0 all-gather.6
  182.8 53.0 all-gather.12
  238.6 62.5 all-gather.14
  304.0 62.3 all-gather.16
  430.6 97.7 reduce-scatter.8
  535.1 176.1 reduce-scatter.6
  717.2 97.9 reduce-scatter.12
  821.7 97.9 reduce-scatter.10
  926.2 134.4 reduce-scatter.14
  1068.1 134.5 reduce-scatter.16
